TPU v7x, 32 devices: a whole 2x2x4 slice. The times are simulated.
32 devices in a mesh: blk: 8 (over y, x, core), grp: 4 (over z).
Axes of the slice: x: 2, y: 2, z: 4, core: 2. Of those that a mesh axis runs over, the one named last changes fastest.
Arguments:
- inverse: bfloat16 [2, 8, 1024, 1024], P(None, 'blk', 'grp'), may hold values from -0.0034375 to 0.1734375
- excite: bfloat16 [2, 8, 1024, 128], P(None, 'blk'), may hold values from -0.125 to 0.125
- coordinates: int32 [3, 8, 1024], replicated, may hold values from 0 to 31, as said below
- block_of_slot: int32 [8], replicated, may hold values from 0 to 7, each once
- panel_order: int32 [8], replicated, may hold values from 0 to 7, each once
Outputs:
- reduced: float32 [2, 1024, 1024], P(None, 'blk', 'grp')
- schur: float32 [2, 1024, 1024], P(None, 'blk', 'grp')
Inputs may be any that keep to these rules, and one draw needn't show every extreme that they name: `coordinates`: components 0 and 1 lie in 0 to 31, component 2 in 0 to 15. No two unknowns of any blocks share a lattice point. `block_of_slot`: slot s is the (s mod 1)-th block of index s // 1 of blk; every block number appears once. `panel_order`: every block number appears once; the first 2 are eliminated in that order, without pivoting.
All inputs are finite; a program needn't handle non-finite values.
Results may differ from a plain program's by a relative error of at most 0.0055.
Values may be sent and summed in bfloat16 or wider, within the bound.
A program may use at most 64 MiB of HBM per device.

v0:
```python
import jax
import jax.numpy as jnp
from jax import lax
from jax.sharding import PartitionSpec as P

PANELS = 2


SELF_REAL = 12.0
SELF_IMAG = -3.0
COUPLE = 2.0
WAVE = 1.3


def from_root(value, axis, source):
    kept = jnp.where(lax.axis_index(axis) == source, value, 0).astype(value.dtype)
    return lax.psum(kept, axis)


def green_tile(test_pos, basis_pos):
    squared = jnp.zeros((test_pos.shape[1], basis_pos.shape[1]), jnp.int32)
    for which in range(3):
        spacing = test_pos[which][:, None] - basis_pos[which][None, :]
        squared = squared + spacing * spacing
    coincide = squared == 0
    distance = jnp.sqrt(jnp.maximum(squared, 1).astype(jnp.float32))
    scaled = COUPLE / distance
    angle_term = WAVE * distance
    real_part = jnp.where(coincide, jnp.float32(SELF_REAL), scaled * jnp.cos(angle_term))
    imag_part = jnp.where(coincide, jnp.float32(SELF_IMAG), -scaled * jnp.sin(angle_term))
    return (real_part.astype(jnp.bfloat16), imag_part.astype(jnp.bfloat16))


def solve_pivot(pivot, right):
    upper_bound = lax.Precision.HIGHEST
    funcs = pivot.shape[1]
    top = jnp.concatenate([pivot[0], -pivot[1]], axis=1)
    lower = jnp.concatenate([pivot[1], pivot[0]], axis=1)
    real_form = jnp.concatenate([top, lower], axis=0)
    stacked = jnp.concatenate([right[0], right[1]], axis=0)
    normal = jnp.dot(real_form.T, real_form, precision=upper_bound)
    factor = jnp.linalg.cholesky(normal)
    answer = jax.scipy.linalg.cho_solve(
        (factor, True), jnp.dot(real_form.T, stacked, precision=upper_bound)
    )
    misfit = stacked - jnp.dot(real_form, answer, precision=upper_bound)
    answer = answer + jax.scipy.linalg.cho_solve(
        (factor, True), jnp.dot(real_form.T, misfit, precision=upper_bound)
    )
    return (answer[:funcs], answer[funcs:])


def on_device(inverse, excite, coordinates, block_of_slot, panel_order):
    upper_bound = lax.Precision.HIGHEST
    per_dev = inverse.shape[1]
    funcs = excite.shape[3]
    blocks = block_of_slot.shape[0]
    block_number = lax.axis_index("blk")
    grp_index = lax.axis_index("grp")
    own_slots = block_number * per_dev + jnp.arange(per_dev, dtype=jnp.int32)
    own_ids = jnp.take(block_of_slot, own_slots)
    rows_real = jnp.einsum(
        "sur,src->suc", inverse[0], excite[0], preferred_element_type=jnp.float32
    ) - jnp.einsum("sur,src->suc", inverse[1], excite[1], preferred_element_type=jnp.float32)
    rows_imag = jnp.einsum(
        "sur,src->suc", inverse[0], excite[1], preferred_element_type=jnp.float32
    ) + jnp.einsum("sur,src->suc", inverse[1], excite[0], preferred_element_type=jnp.float32)
    basis_rows = jnp.stack([rows_real, rows_imag]).astype(jnp.bfloat16)
    own_full = lax.all_gather(basis_rows, "grp", axis=2, tiled=True)
    own_pos = jnp.take(coordinates, own_ids, axis=1)
    sliced = lax.all_gather(basis_rows, "blk", axis=1, tiled=True)
    slot_list = jnp.arange(blocks, dtype=jnp.int32)
    matches = block_of_slot[None, :] == slot_list[:, None]
    slot_of_block = jnp.sum(jnp.where(matches, slot_list[None, :], 0), axis=1)
    grouped_per_block = jnp.take(sliced, slot_of_block, axis=1)
    slab = lax.all_to_all(grouped_per_block, "grp", split_axis=1, concat_axis=2, tiled=True)
    slab_count = slab.shape[1]
    own_test = own_full.astype(jnp.float32)
    start_table = jnp.zeros((2, per_dev * funcs, slab_count * funcs), jnp.float32)

    def one_pair(index, carried):
        test_slot = index // slab_count
        slab_slot = index % slab_count
        test_pos = lax.dynamic_index_in_dim(own_pos, test_slot, 1, keepdims=False)
        basis_pos = lax.dynamic_index_in_dim(
            coordinates, grp_index * slab_count + slab_slot, 1, keepdims=False
        )
        greens_function_real, greens_function_imaginary = green_tile(test_pos, basis_pos)
        basis = lax.dynamic_index_in_dim(slab, slab_slot, 1, keepdims=False)
        product_real = jnp.dot(
            greens_function_real, basis[0], preferred_element_type=jnp.float32
        ) - jnp.dot(greens_function_imaginary, basis[1], preferred_element_type=jnp.float32)
        product_imaginary = jnp.dot(
            greens_function_real, basis[1], preferred_element_type=jnp.float32
        ) + jnp.dot(greens_function_imaginary, basis[0], preferred_element_type=jnp.float32)
        tested = lax.dynamic_index_in_dim(own_test, test_slot, 1, keepdims=False)
        coupled_real = jnp.dot(tested[0].T, product_real, precision=upper_bound) + jnp.dot(
            tested[1].T, product_imaginary, precision=upper_bound
        )
        coupled_imag = jnp.dot(tested[0].T, product_imaginary, precision=upper_bound) - jnp.dot(
            tested[1].T, product_real, precision=upper_bound
        )
        placed = jnp.stack([coupled_real, coupled_imag])
        return lax.dynamic_update_slice(carried, placed, (0, test_slot * funcs, slab_slot * funcs))

    reduced = lax.fori_loop(0, per_dev * slab_count, one_pair, start_table)
    col_blocks = reduced.shape[2] // funcs
    slot_numbers = jnp.arange(blocks, dtype=jnp.int32)
    system_matrix = reduced
    for step in range(PANELS):
        pivot_id = panel_order[step]
        slot_pos = jnp.sum(jnp.where(block_of_slot == pivot_id, slot_numbers, 0))
        owner = slot_pos // per_dev
        local_row = slot_pos % per_dev
        col_owner = pivot_id // col_blocks
        local_col = pivot_id % col_blocks
        upper = system_matrix
        upper = from_root(upper, "blk", owner)
        column = lax.dynamic_slice_in_dim(system_matrix, local_col * funcs, funcs, 2)
        pivot = lax.dynamic_slice_in_dim(upper, local_col * funcs, funcs, 2)
        column, pivot = (from_root(column, "grp", col_owner), from_root(pivot, "grp", col_owner))
        sol_real, sol_imag = solve_pivot(pivot, upper)
        upd_real = jnp.dot(column[0], sol_real, precision=upper_bound) - jnp.dot(
            column[1], sol_imag, precision=upper_bound
        )
        upd_imag = jnp.dot(column[0], sol_imag, precision=upper_bound) + jnp.dot(
            column[1], sol_real, precision=upper_bound
        )
        system_matrix = system_matrix - jnp.stack([upd_real, upd_imag])
    return (reduced, system_matrix)


def solution(mesh):
    placed = (P(None, "blk", "grp", None), P(None, "blk", None, None), P(), P(), P())
    return jax.shard_map(
        on_device,
        mesh=mesh,
        in_specs=placed,
        out_specs=(P(None, "blk", "grp"), P(None, "blk", "grp")),
        check_vma=False,
    )
```

profile of v0, /device:TPU:9, one launch (start us, length us, event | category | flops | bytes accessed | tf_op | source)
XLA Modules:
  0.0 581.7 jit_solution(11726373842314716709)
XLA Ops:
  7.2 1.5 fusion.30
  11.4 25.1 %all-gather.2.cloned.1.call-done = bf16[2,8,256,128]{3,2,1,0:T(8,128)(2,1)} async-done(((bf16[2,1,256,128]{3,2,1,0:T(8,128)(2,1)}), bf16[2,8,256,128]{3,2,1,0:T(8,128)(2,1)}) %all-gather.2.cloned.1.call-update) | async-done | bytes 1048592 | tf_op jit(solution)/shard_map/all_gather | solution.py:71
  36.5 2.0 gather_fusion
  39.6 4.7 all-to-all-start
  45.7 31.6 %all_gather.7 = bf16[2,1,1024,128]{3,2,1,0:T(8,128)(2,1)S(1)} all-gather(bf16[2,1,256,128]{3,2,1,0:T(8,128)(2,1)S(1)} %copy-done.1), channel_id=1, replica_groups=mesh['blk'=8,'grp'=4] {'grp'}, dimensions={2}, use_global_device_ids=true | all-gather | bytes 655360 | tf_op jit(solution)/shard_map/all_gather | solution.py:69
  78.1 1.9 fusion.101
  81.7 168.3 %while.25 = (s32[]{:T(128)}, f32[2,128,256]{2,1,0:T(8,128)S(1)}, s32[3,1,1024]{2,1,0:T(1,128)S(1)}, s32[]{:T(128)}, s32[3,8,1024]{2,1,0:T(8,128)}, /*index=5*/bf...) while((s32[]{:T(128)}, f32[2,128,256]{2,1,0:T(8,128)S(1)}, ...), condition=%wide.region_2.3_spmd, body=%wide.region_1.2_spmd.sunk | while | flops 1948581888 | bytes 9716101 | solution.py:106
  83.1 17.6 %fusion.173 = f32[1024,128]{1,0:T(8,128)S(1)} fusion(bf16[2,2,1024,128]{3,2,1,0:T(8,128)(2,1)S(1)} %get-tuple-element.477, s32[]{:T(128)S(6)} %select_n.290, s32[1024]{0:T(1024)S(1)} %bitcast.272, s32[1024]{0:T(1024)S(1)} %bitcast.280, s32[1024]{0:T(1024)S(1)} %bitcast.268, s32[1024]{0:T(1024)S(1)} %bitcast.276, s32[1024]{0:T(1024)S(1)} %bitcast.264, ...), kind=kOutput, calls=%fused_computation.25.clone.1 | convolution fusion | flops 285212672 | bytes 811012 | tf_op jit(solution)/shard_map/while/body/eval_jaxpr/dot_general | solution.py:90
  100.7 18.2 %convolution_subtract_fusion.18 = f32[1024,128]{1,0:T(8,128)S(1)} fusion(f32[1024,128]{1,0:T(8,128)S(1)} %fusion.173, bf16[2,2,1024,128]{3,2,1,0:T(8,128)(2,1)S(1)} %get-tuple-element.477, s32[]{:T(128)S(6)} %add.355, s32[]{:T(128)S(6)} %select_n.290, s32[1024]{0:T(1024)S(1)} %bitcast.273, s32[1024]{0:T(1024)S(1)} %bitcast.281, ...), kind=kOutput, calls=%fused_computation.8.clone.1 | convolution fusion | flops 286392320 | bytes 1335304 | tf_op jit(solution)/shard_map/while/body/eval_jaxpr/dot_general | solution.py:92
  119.9 17.6 %fusion.171 = f32[1024,128]{1,0:T(8,128)S(1)} fusion(bf16[2,2,1024,128]{3,2,1,0:T(8,128)(2,1)S(1)} %get-tuple-element.477, s32[]{:T(128)S(6)} %add.355, s32[]{:T(128)S(6)} %select_n.290, s32[1024]{0:T(1024)S(1)} %bitcast.274, s32[1024]{0:T(1024)S(1)} %bitcast.282, s32[1024]{0:T(1024)S(1)} %bitcast.270, s32[1024]{0:T(1024)S(1)} %bitcast.278, ...), kind=kOutput, calls=%fused_computation.26.clone.1 | convolution fusion | flops 285212672 | bytes 811016 | tf_op jit(solution)/shard_map/while/body/eval_jaxpr/dot_general | solution.py:93
  137.5 17.9 %convolution_add_fusion.6 = f32[1024,128]{1,0:T(8,128)S(1)} fusion(f32[1024,128]{1,0:T(8,128)S(1)} %fusion.171, bf16[2,2,1024,128]{3,2,1,0:T(8,128)(2,1)S(1)} %get-tuple-element.477, s32[]{:T(128)S(6)} %select_n.290, s32[1024]{0:T(1024)S(1)} %bitcast.275, s32[1024]{0:T(1024)S(1)} %bitcast.283, s32[1024]{0:T(1024)S(1)} %bitcast.271, ...), kind=kOutput, calls=%fused_computation.7.clone.1 | convolution fusion | flops 286392320 | bytes 1335300 | tf_op jit(solution)/shard_map/while/body/eval_jaxpr/dot_general | solution.py:95
  163.0 17.6 %fusion.173 = f32[1024,128]{1,0:T(8,128)S(1)} fusion(bf16[2,2,1024,128]{3,2,1,0:T(8,128)(2,1)S(1)} %get-tuple-element.477, s32[]{:T(128)S(6)} %select_n.290, s32[1024]{0:T(1024)S(1)} %bitcast.272, s32[1024]{0:T(1024)S(1)} %bitcast.280, s32[1024]{0:T(1024)S(1)} %bitcast.268, s32[1024]{0:T(1024)S(1)} %bitcast.276, s32[1024]{0:T(1024)S(1)} %bitcast.264, ...), kind=kOutput, calls=%fused_computation.25.clone.1 | convolution fusion | flops 285212672 | bytes 811012 | tf_op jit(solution)/shard_map/while/body/eval_jaxpr/dot_general | solution.py:90
  180.6 18.1 %convolution_subtract_fusion.18 = f32[1024,128]{1,0:T(8,128)S(1)} fusion(f32[1024,128]{1,0:T(8,128)S(1)} %fusion.173, bf16[2,2,1024,128]{3,2,1,0:T(8,128)(2,1)S(1)} %get-tuple-element.477, s32[]{:T(128)S(6)} %add.355, s32[]{:T(128)S(6)} %select_n.290, s32[1024]{0:T(1024)S(1)} %bitcast.273, s32[1024]{0:T(1024)S(1)} %bitcast.281, ...), kind=kOutput, calls=%fused_computation.8.clone.1 | convolution fusion | flops 286392320 | bytes 1335304 | tf_op jit(solution)/shard_map/while/body/eval_jaxpr/dot_general | solution.py:92
  199.8 17.6 %fusion.171 = f32[1024,128]{1,0:T(8,128)S(1)} fusion(bf16[2,2,1024,128]{3,2,1,0:T(8,128)(2,1)S(1)} %get-tuple-element.477, s32[]{:T(128)S(6)} %add.355, s32[]{:T(128)S(6)} %select_n.290, s32[1024]{0:T(1024)S(1)} %bitcast.274, s32[1024]{0:T(1024)S(1)} %bitcast.282, s32[1024]{0:T(1024)S(1)} %bitcast.270, s32[1024]{0:T(1024)S(1)} %bitcast.278, ...), kind=kOutput, calls=%fused_computation.26.clone.1 | convolution fusion | flops 285212672 | bytes 811016 | tf_op jit(solution)/shard_map/while/body/eval_jaxpr/dot_general | solution.py:93
  217.4 17.9 %convolution_add_fusion.6 = f32[1024,128]{1,0:T(8,128)S(1)} fusion(f32[1024,128]{1,0:T(8,128)S(1)} %fusion.171, bf16[2,2,1024,128]{3,2,1,0:T(8,128)(2,1)S(1)} %get-tuple-element.477, s32[]{:T(128)S(6)} %select_n.290, s32[1024]{0:T(1024)S(1)} %bitcast.275, s32[1024]{0:T(1024)S(1)} %bitcast.283, s32[1024]{0:T(1024)S(1)} %bitcast.271, ...), kind=kOutput, calls=%fused_computation.7.clone.1 | convolution fusion | flops 286392320 | bytes 1335300 | tf_op jit(solution)/shard_map/while/body/eval_jaxpr/dot_general | solution.py:95
  254.1 52.8 %all-reduce.8.cloned.1.call-done = f32[2,128,256]{2,1,0:T(8,128)} async-done(((f32[2,128,256]{2,1,0:T(8,128)}), f32[2,128,256]{2,1,0:T(8,128)}) %all-reduce.8.cloned.1.call-update) | async-done | bytes 262160 | tf_op jit(solution)/shard_map/psum | solution.py:17
  306.8 1.6 dynamic-slice_select_fusion.2
  310.1 34.1 %all-reduce.14.cloned.1.call-done = (f32[2,128,128]{2,1,0:T(8,128)}, f32[2,128,128]{2,1,0:T(8,128)}) async-done(((f32[2,128,128]{2,1,0:T(8,128)}, f32[2,128,128]{2,1,0:T(8,128)}), (f32[2,128,128]{2,1,0:T(8,128)}, f32[2,128,128]{2,1,0:T(8,128)})) %all-reduce.14.cloned.1.call-update) | async-done | bytes 262160 | tf_op jit(solution)/shard_map/psum | solution.py:17
  346.7 11.7 %cholesky.130 = f32[128,128]{1,0:T(8,128)S(1)} custom-call(f32[128,128]{1,0:T(8,128)S(1)} %cholesky.194), custom_call_target="Cholesky" | custom-call | tf_op jit(solution)/shard_map/jit(cholesky)/cholesky | solution.py:42
  358.5 9.8 %custom-call.17 = f32[1,128,128]{1,2,0:T(8,128)S(1)} custom-call(f32[1,128,128]{2,1,0:T(8,128)S(1)} %get-tuple-element.320), custom_call_target="InvertDiagBlocksLowerTriangular" | custom-call | tf_op jit(solution)/shard_map/jit(cholesky)/cholesky | solution.py:42
  368.8 11.7 %cholesky.147 = f32[128,128]{1,0:T(8,128)S(1)} custom-call(f32[128,128]{1,0:T(8,128)S(1)} %convolution_subtract_fusion.16), custom_call_target="Cholesky" | custom-call | tf_op jit(solution)/shard_map/jit(cholesky)/cholesky | solution.py:42
  382.6 4.4 while.26
  383.7 1.4 bitcast_dynamic-update-slice_fusion.4
  387.0 19.7 %custom-call.18 = f32[2,128,128]{1,2,0:T(8,128)S(1)} custom-call(f32[2,128,128]{2,1,0:T(8,128)S(1)} %get-tuple-element.232), custom_call_target="InvertDiagBlocksLowerTriangular" | custom-call | tf_op jit(solution)/shard_map/jit(_cho_solve)/triangular_solve | solution.py:43
  417.2 50.7 %all-reduce.10.cloned.1.call-done = f32[2,128,256]{2,1,0:T(8,128)} async-done(((f32[2,128,256]{2,1,0:T(8,128)}), f32[2,128,256]{2,1,0:T(8,128)}) %all-reduce.10.cloned.1.call-update) | async-done | bytes 262160 | tf_op jit(solution)/shard_map/psum | solution.py:17
  467.9 1.6 dynamic-slice_select_fusion
  470.5 34.6 %all-reduce.12.cloned.1.call-done = (f32[2,128,128]{2,1,0:T(8,128)}, f32[2,128,128]{2,1,0:T(8,128)}) async-done(((f32[2,128,128]{2,1,0:T(8,128)}, f32[2,128,128]{2,1,0:T(8,128)}), (f32[2,128,128]{2,1,0:T(8,128)}, f32[2,128,128]{2,1,0:T(8,128)})) %all-reduce.12.cloned.1.call-update) | async-done | bytes 262160 | tf_op jit(solution)/shard_map/psum | solution.py:17
  507.6 11.7 %cholesky.164 = f32[128,128]{1,0:T(8,128)S(1)} custom-call(f32[128,128]{1,0:T(8,128)S(1)} %cholesky.197), custom_call_target="Cholesky" | custom-call | tf_op jit(solution)/shard_map/jit(cholesky)/cholesky | solution.py:42
  519.4 9.8 %custom-call.20 = f32[1,128,128]{1,2,0:T(8,128)S(1)} custom-call(f32[1,128,128]{2,1,0:T(8,128)S(1)} %get-tuple-element.316), custom_call_target="InvertDiagBlocksLowerTriangular" | custom-call | tf_op jit(solution)/shard_map/jit(cholesky)/cholesky | solution.py:42
  529.7 11.7 %cholesky.181 = f32[128,128]{1,0:T(8,128)S(1)} custom-call(f32[128,128]{1,0:T(8,128)S(1)} %convolution_subtract_fusion.15), custom_call_target="Cholesky" | custom-call | tf_op jit(solution)/shard_map/jit(cholesky)/cholesky | solution.py:42
  544.1 4.2 while.27
  548.2 19.7 %custom-call.21 = f32[2,128,128]{1,2,0:T(8,128)S(1)} custom-call(f32[2,128,128]{2,1,0:T(8,128)S(1)} %get-tuple-element.234), custom_call_target="InvertDiagBlocksLowerTriangular" | custom-call | tf_op jit(solution)/shard_map/jit(_cho_solve)/triangular_solve | solution.py:43
  (147 shorter events, 49.1 us)
Async XLA Ops:
  7.2 1.6 copy-start.6
  7.2 2.8 copy-start.7
  7.2 29.3 %all-gather.2.cloned.1.call-start = ((), (), s32[]{:S(2)}) async-start(), calls=%async_computation.1 | async-start | bytes 1179648 | tf_op jit(solution)/shard_map/all_gather | solution.py:71
  10.0 1.3 copy-start.5
  39.6 6.1 %copy-start.1 = (bf16[2,1,256,128]{3,2,1,0:T(8,128)(2,1)S(1)}, bf16[2,1,256,128]{3,2,1,0:T(8,128)(2,1)}, u32[]{:S(2)}) copy-start(bf16[2,1,256,128]{3,2,1,0:T(8,128)(2,1)} %pad_maximum_fusion.9) | copy-start | bytes 393220
  39.6 41.9 %all-to-all-start = ((bf16[2,8,256,128]{3,2,0,1:T(8,128)(2,1)}), bf16[2,8,256,128]{3,2,0,1:T(8,128)(2,1)S(1)}, u32[]{:S(2)}, u32[]{:S(2)}) async-start(bf16[2,8,256,128]{3,2,0,1:T(8,128)(2,1)} %select_bitcast_fusion), calls=%async_computation | async-start | bytes 2097152 | tf_op jit(solution)/shard_map/all_to_all | solution.py:76
  44.3 262.5 %all-reduce.8.cloned.1.call-start = ((), (), s32[]{:S(2)}) async-start(), calls=%async_computation.2 | async-start | bytes 524288 | tf_op jit(solution)/shard_map/psum | solution.py:17
  45.7 31.7 %copy-start.4 = (s32[8]{0:T(128)S(1)}, s32[8]{0:T(128)}, u32[]{:S(2)}) copy-start(s32[8]{0:T(128)} %param.14) | copy-start | bytes 100
  250.0 162.9 %copy-start = (f32[2,128,256]{2,1,0:T(8,128)}, f32[2,128,256]{2,1,0:T(8,128)S(1)}, u32[]{:S(2)}) copy-start(f32[2,128,256]{2,1,0:T(8,128)S(1)} %get-tuple-element.252) | copy-start | bytes 786436
  250.9 93.4 %all-reduce.14.cloned.1.call-start = ((), (), s32[]{:S(2)}) async-start(), calls=%async_computation.5 | async-start | bytes 524288 | tf_op jit(solution)/shard_map/psum | solution.py:17
  308.4 159.5 %all-reduce.10.cloned.1.call-start = ((), (), s32[]{:S(2)}) async-start(), calls=%async_computation.3 | async-start | bytes 524288 | tf_op jit(solution)/shard_map/psum | solution.py:17
  410.7 1.2 copy-start.2
  413.8 91.3 %all-reduce.12.cloned.1.call-start = ((), (), s32[]{:S(2)}) async-start(), calls=%async_computation.4 | async-start | bytes 524288 | tf_op jit(solution)/shard_map/psum | solution.py:17
  571.9 1.2 copy-start.3
Sparse Core Ops, SparseCore 0:
  11.4 25.0 all-gather.1
  251.0 55.8 all-reduce.7
  309.9 34.2 all-reduce.13
  413.9 53.9 all-reduce.9
  470.8 34.2 all-reduce.11
where the time goes:
time: 588 us; the launch traced here: 582 us
  waiting for transfers between devices  197 us (34%)
  matrix products  168 us (29%)
  other arithmetic  121 us (21%)
  blocking collectives  31.6 us (5%)
  between operations  24.2 us (4%)
  local copies, waits for them, and re-layouts  17.2 us (3%)
  loops' own time  16.5 us (3%)
    psum x4, waiting for transfers between devices, from_root(): return lax.psum(kept, axis)  172 us
    another operation x13, other arithmetic, solve_pivot(): factor = jnp.linalg.cholesky(normal)  68.5 us
    another operation x5, other arithmetic, solve_pivot(): jax.scipy.linalg.cho_solve((factor, True), jnp.dot(real_form.T, stacked,...  39.4 us
    dot_general x2, matrix products, one_pair(): jnp.dot(greens_function_imaginary, basis[1], preferred_element_type=jnp.f...  36.3 us
    dot_general x2, matrix products, one_pair(): jnp.dot(greens_function_imaginary, basis[0], preferred_element_type=jnp.f...  35.8 us
    dot_general x2, matrix products, one_pair(): jnp.dot(greens_function_real, basis[0], preferred_element_type=jnp.float32)  35.2 us
    dot_general x2, matrix products, one_pair(): jnp.dot(greens_function_real, basis[1], preferred_element_type=jnp.float32)  35.2 us
    all_gather x1, blocking collectives, on_device(): own_full = lax.all_gather(basis_rows, 'grp', axis=2, tiled=True)  31.6 us
  transfers between devices with their start and end apart: 6, of which 5 were waited for; matrix products, arithmetic and copies ran while one was open for 1% of the time, Pallas kernels for 0%

commit v1 on v0

v1 whole, which is shorter than its diff:
```python
import functools

import jax
import jax.numpy as jnp
from jax import lax
from jax.experimental import pallas as pl
from jax.experimental.pallas import tpu as pltpu
from jax.sharding import PartitionSpec as P

PANELS = 2

SELF_REAL = 12.0
SELF_IMAG = -3.0
COUPLE = 2.0
WAVE = 1.3

COS_TURN = (0.999999211770312, -19.738980419471126, 64.92865850463285, -85.27162830146948,
            58.79050662870376, -21.071108461771125)
SIN_TURN = (6.283184916984331, -41.34158926418157, 81.59994386455666, -76.61447586020026,
            41.342889428722025, -12.471244745942547)
TURNS = WAVE / (2.0 * 3.141592653589793)

HIGH = lax.Precision.HIGHEST


def horner(coefs, x):
    total = jnp.full_like(x, coefs[-1])
    for c in coefs[-2::-1]:
        total = total * x + c
    return total


def green_kernel(test_ref, basis_ref, out_ref):
    rows = out_ref.shape[1]
    unk = basis_ref.shape[2]
    chunk = 16

    def body(i, _):
        start = pl.multiple_of(i * chunk, chunk)
        test = test_ref[pl.ds(start, chunk), :]
        squared = None
        for which in range(3):
            spacing = test[:, which:which + 1] - basis_ref[0, which:which + 1, :]
            term = spacing * spacing
            squared = term if squared is None else squared + term
        coincide = squared == 0.0
        bounded = jnp.maximum(squared, 1.0)
        inverted = lax.rsqrt(bounded)
        turns = bounded * inverted * TURNS
        frac = turns - jnp.floor(turns + 0.5)
        frac2 = frac * frac
        scaled = COUPLE * inverted
        real = jnp.where(coincide, SELF_REAL, scaled * horner(COS_TURN, frac2))
        imag = jnp.where(coincide, SELF_IMAG, -(scaled * frac) * horner(SIN_TURN, frac2))
        out_ref[0, pl.ds(start, chunk), :unk] = real.astype(jnp.bfloat16)
        out_ref[0, pl.ds(start, chunk), unk:] = imag.astype(jnp.bfloat16)
        return 0

    lax.fori_loop(0, rows // chunk, body, 0)


def green_tiles(test_pos, basis_pos):
    unk = test_pos.shape[0]
    slab = basis_pos.shape[0]
    rows = min(256, unk)
    return pl.pallas_call(
        green_kernel,
        grid=(slab, unk // rows),
        in_specs=[
            pl.BlockSpec((rows, 3), lambda s, i: (i, 0)),
            pl.BlockSpec((1, 3, unk), lambda s, i: (s, 0, 0)),
        ],
        out_specs=pl.BlockSpec((1, rows, 2 * unk), lambda s, i: (s, i, 0)),
        out_shape=jax.ShapeDtypeStruct((slab, unk, 2 * unk), jnp.bfloat16),
        cost_estimate=pl.CostEstimate(
            flops=slab * unk * unk * 6000, bytes_accessed=slab * unk * unk * 4, transcendentals=slab * unk * unk
        ),
        name="green",
    )(test_pos, basis_pos)


def couple_kernel(green_ref, basis_ref, tested_ref, out_ref):
    real, imag = basis_ref[0, 0], basis_ref[1, 0]
    funcs = real.shape[1]
    top = jnp.concatenate([real, imag], axis=1)
    low = jnp.concatenate([-imag, real], axis=1)
    packed = jnp.concatenate([top, low], axis=0)
    product = jnp.dot(green_ref[0], packed, preferred_element_type=jnp.float32)
    high = product.astype(jnp.bfloat16)
    rest = (product - high.astype(jnp.float32)).astype(jnp.bfloat16)
    tested = tested_ref[...]
    outer = jnp.dot(tested, high, preferred_element_type=jnp.float32) + jnp.dot(
        tested, rest, preferred_element_type=jnp.float32
    )
    out_ref[0] = outer[:funcs, :funcs] + outer[funcs:, funcs:]
    out_ref[1] = outer[:funcs, funcs:] - outer[funcs:, :funcs]


def couple(green, slab_basis, tested):
    slab, unk, _ = green.shape
    funcs = slab_basis.shape[3]
    return pl.pallas_call(
        couple_kernel,
        grid=(slab,),
        in_specs=[
            pl.BlockSpec((1, unk, 2 * unk), lambda s: (s, 0, 0)),
            pl.BlockSpec((2, 1, unk, funcs), lambda s: (0, s, 0, 0)),
            pl.BlockSpec((2 * funcs, unk), lambda s: (0, 0)),
        ],
        out_specs=pl.BlockSpec((2, funcs, funcs), lambda s: (0, 0, s)),
        out_shape=jax.ShapeDtypeStruct((2, funcs, slab * funcs), jnp.float32),
        compiler_params=pltpu.CompilerParams(vmem_limit_bytes=40 * 1024 * 1024),
        cost_estimate=pl.CostEstimate(
            flops=slab * unk * unk * funcs * 8, bytes_accessed=slab * unk * unk * 4, transcendentals=0
        ),
        name="couple",
    )(green, slab_basis, tested)


def cdot(a, b):
    m, n = a[0].shape[0], b[0].shape[1]
    left = jnp.concatenate(a, axis=0)
    right = jnp.concatenate(b, axis=1)
    outer = jnp.dot(left, right, precision=HIGH, preferred_element_type=jnp.float32)
    return (outer[:m, :n] - outer[m:, n:], outer[:m, n:] + outer[m:, :n])


def csub(a, b):
    return (a[0] - b[0], a[1] - b[1])


def cadd(a, b):
    return (a[0] + b[0], a[1] + b[1])


def hermitian_inverse(herm):
    n = herm[0].shape[0]
    group = 8
    lane = lax.broadcasted_iota(jnp.int32, (1, n), 1)
    sub = lax.broadcasted_iota(jnp.int32, (group, 1), 0)

    def turn(_, carried):
        real, imag = carried
        head_r, head_i = real[:group], imag[:group]
        tail_r, tail_i = real[group:], imag[group:]
        for j in range(group):
            here = lane == j
            mine = sub == j
            row_r, row_i = head_r[j:j + 1, :], head_i[j:j + 1, :]
            scale = 1.0 / row_r[:, j:j + 1]
            row_r = jnp.where(here, 1.0, row_r) * scale
            row_i = jnp.where(here, 0.0, row_i) * scale
            col_r, col_i = tail_r[:, j:j + 1], tail_i[:, j:j + 1]
            tail_r = jnp.where(here, 0.0, tail_r) - col_r * row_r + col_i * row_i
            tail_i = jnp.where(here, 0.0, tail_i) - col_r * row_i - col_i * row_r
            col_r = jnp.where(mine, -1.0, head_r[:, j:j + 1])
            col_i = jnp.where(mine, 0.0, head_i[:, j:j + 1])
            gone = here | mine
            head_r = jnp.where(gone, 0.0, head_r) - col_r * row_r + col_i * row_i
            head_i = jnp.where(gone, 0.0, head_i) - col_r * row_i - col_i * row_r
        real = pltpu.roll(jnp.concatenate([tail_r, head_r], axis=0), n - group, 1)
        imag = pltpu.roll(jnp.concatenate([tail_i, head_i], axis=0), n - group, 1)
        return real, imag

    return lax.fori_loop(0, n // group, turn, herm)


def inverse_of(d):
    n = d[0].shape[0]
    adjoint = (d[0].T, -d[1].T)
    guess = cdot(hermitian_inverse(cdot(adjoint, d)), adjoint)
    off = cdot(d, guess)
    row = lax.broadcasted_iota(jnp.int32, (n, n), 0)
    col = lax.broadcasted_iota(jnp.int32, (n, n), 1)
    unit = jnp.where(row == col, 1.0, 0.0)
    return cadd(guess, cdot(guess, (unit - off[0], -off[1])))


def pivot_kernel(d_ref, first_ref, joint_ref, second_ref):
    def tile(i, j):
        return (d_ref[i, j, 0], d_ref[i, j, 1])

    first = inverse_of(tile(0, 0))
    joint = cdot(first, tile(0, 1))
    second = inverse_of(csub(tile(1, 1), cdot(tile(1, 0), joint)))
    for ref, value in ((first_ref, first), (joint_ref, joint), (second_ref, second)):
        ref[0] = value[0]
        ref[1] = value[1]


def pivot_inverses(pivots):
    funcs = pivots.shape[3]
    shape = jax.ShapeDtypeStruct((2, funcs, funcs), jnp.float32)
    return pl.pallas_call(
        pivot_kernel,
        out_shape=(shape, shape, shape),
        compiler_params=pltpu.CompilerParams(vmem_limit_bytes=32 * 1024 * 1024),
        cost_estimate=pl.CostEstimate(flops=20_000_000_000, bytes_accessed=1_000_000, transcendentals=0),
        name="pivots",
    )(pivots)


def update_kernel(full_ref, rows_ref, cols_ref, low_ref, first_ref, joint_ref, second_ref, out_ref):
    def pair(ref):
        return (ref[0], ref[1])

    upper0 = (rows_ref[0, 0], rows_ref[0, 1])
    upper1 = (rows_ref[1, 0], rows_ref[1, 1])
    begun = cdot(pair(first_ref), upper0)
    sol1 = cdot(pair(second_ref), csub(upper1, cdot(pair(low_ref), begun)))
    sol0 = csub(begun, cdot(pair(joint_ref), sol1))
    taken = cadd(
        cdot((cols_ref[0, 0], cols_ref[0, 1]), sol0), cdot((cols_ref[1, 0], cols_ref[1, 1]), sol1)
    )
    out_ref[0] = full_ref[0] - taken[0]
    out_ref[1] = full_ref[1] - taken[1]


def update(full, rows, cols, low, first, joint, second):
    return pl.pallas_call(
        update_kernel,
        out_shape=jax.ShapeDtypeStruct(full.shape, jnp.float32),
        compiler_params=pltpu.CompilerParams(vmem_limit_bytes=32 * 1024 * 1024),
        cost_estimate=pl.CostEstimate(flops=2_000_000_000, bytes_accessed=2_000_000, transcendentals=0),
        name="update",
    )(full, rows, cols, low, first, joint, second)


def on_device(inverse, excite, coordinates, block_of_slot, panel_order):
    funcs = excite.shape[3]
    blocks = block_of_slot.shape[0]
    grp_index = lax.axis_index("grp")
    slab_count = blocks // lax.axis_size("grp")
    own_id = block_of_slot[lax.axis_index("blk")]

    exc_r, exc_i = excite[0, 0], excite[1, 0]
    right_r = jnp.concatenate([exc_r, exc_i], axis=1)
    right_i = jnp.concatenate([-exc_i, exc_r], axis=1)
    rows = jnp.dot(inverse[0, 0], right_r, preferred_element_type=jnp.float32) + jnp.dot(
        inverse[1, 0], right_i, preferred_element_type=jnp.float32
    )
    basis_rows = jnp.stack([rows[:, :funcs], rows[:, funcs:]]).astype(jnp.bfloat16)[:, None]

    places = coordinates.astype(jnp.float32)
    own_pos = lax.dynamic_index_in_dim(places, own_id, 1, keepdims=False).T
    slab_pos = lax.dynamic_slice_in_dim(places, grp_index * slab_count, slab_count, 1)
    green = green_tiles(own_pos, jnp.transpose(slab_pos, (1, 0, 2)))

    sliced = lax.all_gather(basis_rows, "blk", axis=1, tiled=True)
    slots = jnp.arange(blocks, dtype=jnp.int32)
    grouped = jnp.concatenate(
        [
            lax.dynamic_slice_in_dim(sliced, jnp.sum(jnp.where(block_of_slot == b, slots, 0)), 1, 1)
            for b in range(blocks)
        ],
        axis=1,
    )
    slab = lax.all_to_all(grouped, "grp", split_axis=1, concat_axis=2, tiled=True)
    own_full = lax.all_gather(basis_rows, "grp", axis=2, tiled=True)[:, 0]
    tested = jnp.transpose(own_full, (0, 2, 1)).reshape(2 * funcs, -1)

    reduced = couple(green, slab, tested)

    row_mine = [own_id == panel_order[q] for q in range(PANELS)]
    col_mine = [panel_order[q] // slab_count == grp_index for q in range(PANELS)]
    cols = jnp.stack([
        jnp.where(
            col_mine[q],
            lax.dynamic_slice_in_dim(reduced, (panel_order[q] % slab_count) * funcs, funcs, 2),
            0.0,
        )
        for q in range(PANELS)
    ])
    pivots = jnp.stack([jnp.where(row_mine[q], cols, 0.0) for q in range(PANELS)])
    pivots = lax.psum(pivots, ("blk", "grp"))
    upper = lax.psum(jnp.stack([jnp.where(row_mine[q], reduced, 0.0) for q in range(PANELS)]), "blk")
    cols = lax.psum(cols, "grp")
    first, joint, second = pivot_inverses(pivots)
    schur = update(reduced, upper, cols, pivots[1, 0], first, joint, second)
    return (reduced, schur)


def solution(mesh):
    placed = (P(None, "blk", "grp", None), P(None, "blk", None, None), P(), P(), P())
    return jax.shard_map(
        on_device,
        mesh=mesh,
        in_specs=placed,
        out_specs=(P(None, "blk", "grp"), P(None, "blk", "grp")),
        check_vma=False,
    )
```

time: 588 us -> 367 us (0.62)
  matrix products: 168 us -> 2.79 us
  other arithmetic: 121 us -> 8.54 us
  Pallas kernels: 0 us -> 71.6 us
  loops' own time: 16.5 us -> 0 us
  between operations: 24.2 us -> 38.4 us
  waiting for transfers between devices: 197 us -> 185 us
    dot_general x36 -> x2, matrix products: 160 us -> 2.79 us  [the longest x1 1.4 us: on_device(): jnp.dot(inverse[0, 0], right_r, preferred_element_type=jnp.float32)]
    another operation x21 -> x6, other arithmetic: 109 us -> 5.08 us  [the longest x2 1.84 us: on_device(): jnp.stack([jnp.where(row_mine[q], reduced, 0.0) for q in range(PANELS)])]
    pallas_call x0 -> x4, Pallas kernels: none -> 71.6 us  [the longest x1 37 us: pivot_inverses(): pl.pallas_call(pivot_kernel, out_shape=(shape, shape, shape), compiler_pa...]
    all_gather x1, waiting for transfers between devices: 25.1 us -> 0.02 us  [on_device(): sliced = lax.all_gather(basis_rows, 'blk', axis=1, tiled=True)]
    another operation x3 -> x0, loops' own time: 16.5 us -> none  [the longest x1 15.7 us: on_device(): reduced = lax.fori_loop(0, per_dev * slab_count, one_pair, start_table)]
    unnamed x16 -> x17, local copies, waits for them, and re-layouts: 0.04 us -> 12.9 us
    psum x4 -> x3, waiting for transfers between devices: 172 us -> 185 us  [the longest x1 127 us: on_device(): pivots = lax.psum(pivots, ('blk', 'grp'))]
    select_n x9 -> x1, other arithmetic: 8.05 us -> 0.04 us  [on_device(): jnp.where(row_mine[q], cols, 0.0)]
  transfers between devices with their start and end apart: 6 -> 5, of which waited for: 5 -> 2; matrix products, arithmetic and copies ran while one was open for 1% -> 3% of each run, Pallas kernels for 0% -> 17%
where the time goes in v1:
time: 367 us; the launch traced here: 364 us
  waiting for transfers between devices  185 us (50%)
  Pallas kernels  71.6 us (20%)
  between operations  38.4 us (10%)
  blocking collectives  31.3 us (9%)
  local copies, waits for them, and re-layouts  20.9 us (6%)
  other arithmetic  8.54 us (2%)
  starting transfers between devices  5.06 us (1%)
    psum x1, waiting for transfers between devices, on_device(): pivots = lax.psum(pivots, ('blk', 'grp'))  127 us
    psum x1, waiting for transfers between devices, on_device(): lax.psum(jnp.stack([jnp.where(row_mine[q], reduced, 0.0) for q in range(P...  57.7 us
    pallas_call x1, Pallas kernels, pivot_inverses(): pl.pallas_call(pivot_kernel, out_shape=(shape, shape, shape), compiler_pa...  37 us
    all_gather x1, blocking collectives, on_device(): own_full = lax.all_gather(basis_rows, 'grp', axis=2, tiled=True)[:, 0]  31.3 us
    pallas_call x1, Pallas kernels, green_tiles(): pl.pallas_call(green_kernel, grid=(slab, unk // rows), in_specs=[pl.Block...  23.6 us
    unnamed x17, local copies, waits for them, and re-layouts  12.9 us
  transfers between devices with their start and end apart: 5, of which 2 were waited for; matrix products, arithmetic and copies ran while one was open for 3% of the time, Pallas kernels for 17%

profile of v1, /device:TPU:9, one launch (start us, length us, event | category | flops | bytes accessed | tf_op | source)
XLA Modules:
  0.0 363.7 jit_solution(15333198356799395823)
XLA Ops:
  7.2 1.1 slice_bitcast_fusion.1
  8.3 1.0 fusion.29
  9.3 1.4 fusion.2
  10.7 1.4 fusion.1
  12.8 1.5 fusion.26
  24.3 1.2 dynamic_slice.40
  26.8 1.3 fusion.30
  41.4 1.0 copy_convert_fusion
  42.4 0.9 dynamic-slice_dynamic-update-slice_fusion.7
  43.3 0.9 dynamic-slice_dynamic-update-slice_fusion.6
  44.2 0.9 dynamic-slice_dynamic-update-slice_fusion.5
  45.2 0.9 dynamic-slice_dynamic-update-slice_fusion.4
  46.1 0.9 dynamic-slice_dynamic-update-slice_fusion.3
  47.0 0.9 dynamic-slice_dynamic-update-slice_fusion.2
  47.9 0.9 dynamic-slice_dynamic-update-slice_fusion.1
  48.9 0.9 dynamic-slice_dynamic-update-slice_fusion
  49.8 1.1 copy.14
  50.9 4.8 %all-to-all-start = ((bf16[2,8,256,128]{2,3,0,1:T(8,128)(2,1)}), bf16[2,8,256,128]{2,3,0,1:T(8,128)(2,1)S(1)}, u32[]{:S(2)}, u32[]{:S(2)}) async-start(bf16[2,8,256,128]{2,3,0,1:T(8,128)(2,1)} %copy.14), calls=%async_computation | async-start | bytes 2097152 | tf_op jit(solution)/shard_map/all_to_all | solution.py:258
  55.7 1.0 copy.13
  57.3 31.3 %all_gather.7 = bf16[2,1,1024,128]{2,3,1,0:T(8,128)(2,1)S(1)} all-gather(bf16[2,1,256,128]{2,3,1,0:T(8,128)(2,1)} %pad_maximum_fusion.4), channel_id=1, replica_groups=mesh['blk'=8,'grp'=4] {'grp'}, dimensions={2}, use_global_device_ids=true | all-gather | bytes 655360 | tf_op jit(solution)/shard_map/all_gather | solution.py:259
  88.6 23.6 %green.1.green_ref = bf16[2,1024,2048]{2,1,0:T(8,128)(2,1)} custom-call(f32[1024,3]{1,0:T(8,128)} %bitcast.52, f32[2,3,1024]{2,1,0:T(4,128)} %dynamic-slice_bitcast_fusion.basis_ref), custom_call_target="tpu_custom_call" | custom-call | flops 12582912000 | bytes 8388608 | tf_op jit(solution)/shard_map/green/pallas_call | solution.py:66
  112.9 3.4 copy-done
  116.3 4.7 %couple.1.full_ref = f32[2,128,256]{2,1,0:T(8,128)} custom-call(bf16[2,1024,2048]{2,1,0:T(8,128)(2,1)S(1)} %copy-done, bf16[2,2,1024,128]{3,2,1,0:T(8,128)(2,1)S(1)} %bitcast.49, bf16[256,1024]{1,0:T(8,128)(2,1)S(1)} %bitcast.50), custom_call_target="tpu_custom_call" | custom-call | flops 2147483648 | bytes 8388608 | tf_op jit(solution)/shard_map/couple/pallas_call | solution.py:102
  121.0 1.0 fusion.15
  124.0 1.0 select_bitcast_fusion.1
  125.9 127.2 %all-reduce.8.cloned.1.call-done.d_ref = f32[2,2,2,128,128]{4,3,2,1,0:T(8,128)} async-done(((f32[2,2,2,128,128]{4,3,2,1,0:T(8,128)}), f32[2,2,2,128,128]{4,3,2,1,0:T(8,128)}) %all-reduce.8.cloned.1.call-update) | async-done | bytes 524304 | tf_op jit(solution)/shard_map/psum | solution.py:275
  253.1 1.0 copy-done.2
  254.1 37.0 %pivots.1 = (f32[2,128,128]{2,1,0:T(8,128)S(1)}, f32[2,128,128]{2,1,0:T(8,128)S(1)}, f32[2,128,128]{2,1,0:T(8,128)S(1)}) custom-call(f32[2,2,2,128,128]{4,3,2,1,0:T(8,128)S(1)} %copy-done.2), custom_call_target="tpu_custom_call" | custom-call | flops 20000000000 | bytes 1000000 | tf_op jit(solution)/shard_map/pivots/pallas_call | solution.py:194
  291.2 57.7 %all-reduce.4.cloned.1.call-done.rows_ref = f32[2,2,128,256]{3,2,1,0:T(8,128)} async-done(((f32[2,2,128,256]{3,2,1,0:T(8,128)}), f32[2,2,128,256]{3,2,1,0:T(8,128)}) %all-reduce.4.cloned.1.call-update) | async-done | bytes 524304 | tf_op jit(solution)/shard_map/psum | solution.py:276
  349.0 1.0 copy-done.3
  350.0 0.9 copy-done.4
  350.9 6.2 %update.1 = f32[2,128,256]{2,1,0:T(8,128)} custom-call(f32[2,128,256]{2,1,0:T(8,128)S(1)} %copy-done.1, f32[2,2,128,256]{3,2,1,0:T(8,128)S(1)} %copy-done.3, f32[2,2,128,128]{3,2,1,0:T(8,128)S(1)} %copy-done.4, f32[2,128,128]{2,1,0:T(8,128)S(1)} %slice_bitcast_fusion.2.low_ref, f32[2,128,128]{2,1,0:T(8,128)S(1)} %get-tuple-element.5.first_ref, ...), custom_call_target="tpu_custom_call" | custom-call | flops 2000000000 | bytes 2000000 | tf_op jit(solution)/shard_map/update/pallas_call | solution.py:220
  (27 shorter events, 4.9 us)
Async XLA Ops:
  7.2 35.2 %all-gather.2.cloned.1.call-start = ((), (), s32[]{:S(2)}) async-start(), calls=%async_computation.1 | async-start | bytes 1179648 | tf_op jit(solution)/shard_map/all_gather | solution.py:249
  50.9 61.3 %all-to-all-start = ((bf16[2,8,256,128]{2,3,0,1:T(8,128)(2,1)}), bf16[2,8,256,128]{2,3,0,1:T(8,128)(2,1)S(1)}, u32[]{:S(2)}, u32[]{:S(2)}) async-start(bf16[2,8,256,128]{2,3,0,1:T(8,128)(2,1)} %copy.14), calls=%async_computation | async-start | bytes 2097152 | tf_op jit(solution)/shard_map/all_to_all | solution.py:258
  55.7 197.4 %all-reduce.8.cloned.1.call-start = ((), (), s32[]{:S(2)}) async-start(), calls=%async_computation.4 | async-start | bytes 1048576 | tf_op jit(solution)/shard_map/psum | solution.py:275
  112.9 3.4 copy-start
  123.0 168.3 %all-reduce.6.cloned.1.call-start = ((), (), s32[]{:S(2)}) async-start(), calls=%async_computation.3 | async-start | bytes 524288 | tf_op jit(solution)/shard_map/psum | solution.py:277
  123.7 225.2 %all-reduce.4.cloned.1.call-start = ((), (), s32[]{:S(2)}) async-start(), calls=%async_computation.2 | async-start | bytes 1048576 | tf_op jit(solution)/shard_map/psum | solution.py:276
  125.9 223.1 %copy-start.1 = (f32[2,128,256]{2,1,0:T(8,128)S(1)}, f32[2,128,256]{2,1,0:T(8,128)}, u32[]{:S(2)}) copy-start(f32[2,128,256]{2,1,0:T(8,128)} %couple.1.full_ref) | copy-start | bytes 786436
  253.1 1.0 copy-start.2
  349.0 1.0 copy-start.3
  350.0 0.9 copy-start.4
Sparse Core Ops, SparseCore 0:
  12.9 25.0 all-gather.1
  123.1 129.9 all-reduce.7
  256.1 34.7 all-reduce.5
  293.8 55.0 all-reduce.3

commit v2 on v1

--- a/solution.py
+++ b/solution.py
@@ -28,6 +28,57 @@
     for c in coefs[-2::-1]:
         total = total * x + c
     return total
+
+
+def gather_kernel(axis, peers, count, *refs):
+    sources, targets = refs[:count], refs[count:2 * count]
+    send_sem, recv_sem, local_sem = refs[2 * count:]
+    me = lax.axis_index(axis)
+    barrier = pltpu.get_barrier_semaphore()
+    for step in range(1, peers):
+        pl.semaphore_signal(
+            barrier, inc=1, device_id={axis: lax.rem(me + step, peers)}, device_id_type=pl.DeviceIdType.MESH
+        )
+    pl.semaphore_wait(barrier, peers - 1)
+
+    def sent(which, step):
+        return pltpu.make_async_remote_copy(
+            src_ref=sources[which],
+            dst_ref=targets[which].at[me],
+            send_sem=send_sem.at[which, step - 1],
+            recv_sem=recv_sem.at[which, step - 1],
+            device_id={axis: lax.rem(me + step, peers)},
+            device_id_type=pl.DeviceIdType.MESH,
+        )
+
+    copies = [sent(which, step) for step in range(1, peers) for which in range(count)]
+    kept = [
+        pltpu.make_async_copy(sources[which], targets[which].at[me], local_sem.at[which])
+        for which in range(count)
+    ]
+    for copy in copies + kept:
+        copy.start()
+    for copy in kept + copies:
+        copy.wait()
+
+
+def gather(axis, collective_id, *values):
+    peers = lax.axis_size(axis)
+    count = len(values)
+    anywhere = pl.BlockSpec(memory_space=pl.ANY)
+    return pl.pallas_call(
+        functools.partial(gather_kernel, axis, peers, count),
+        in_specs=[anywhere] * count,
+        out_specs=[anywhere] * count,
+        out_shape=[jax.ShapeDtypeStruct((peers,) + v.shape, v.dtype) for v in values],
+        scratch_shapes=[
+            pltpu.SemaphoreType.DMA((count, peers - 1)),
+            pltpu.SemaphoreType.DMA((count, peers - 1)),
+            pltpu.SemaphoreType.DMA((count,)),
+        ],
+        compiler_params=pltpu.CompilerParams(collective_id=collective_id, has_side_effects=True),
+        name="gather_" + axis + str(collective_id),
+    )(*values)
 
 
 def green_kernel(test_ref, basis_ref, out_ref):
@@ -239,42 +290,42 @@
     rows = jnp.dot(inverse[0, 0], right_r, preferred_element_type=jnp.float32) + jnp.dot(
         inverse[1, 0], right_i, preferred_element_type=jnp.float32
     )
-    basis_rows = jnp.stack([rows[:, :funcs], rows[:, funcs:]]).astype(jnp.bfloat16)[:, None]
+    basis_rows = jnp.stack([rows[:, :funcs], rows[:, funcs:]]).astype(jnp.bfloat16)
 
     places = coordinates.astype(jnp.float32)
     own_pos = lax.dynamic_index_in_dim(places, own_id, 1, keepdims=False).T
     slab_pos = lax.dynamic_slice_in_dim(places, grp_index * slab_count, slab_count, 1)
     green = green_tiles(own_pos, jnp.transpose(slab_pos, (1, 0, 2)))
 
-    sliced = lax.all_gather(basis_rows, "blk", axis=1, tiled=True)
+    (sliced,) = gather("blk", 0, basis_rows)
+    (whole,) = gather("grp", 1, basis_rows)
     slots = jnp.arange(blocks, dtype=jnp.int32)
+
+    def slot_of(block):
+        return jnp.sum(jnp.where(block_of_slot == block, slots, 0))
+
     grouped = jnp.concatenate(
-        [
-            lax.dynamic_slice_in_dim(sliced, jnp.sum(jnp.where(block_of_slot == b, slots, 0)), 1, 1)
-            for b in range(blocks)
-        ],
-        axis=1,
-    )
-    slab = lax.all_to_all(grouped, "grp", split_axis=1, concat_axis=2, tiled=True)
-    own_full = lax.all_gather(basis_rows, "grp", axis=2, tiled=True)[:, 0]
-    tested = jnp.transpose(own_full, (0, 2, 1)).reshape(2 * funcs, -1)
+        [lax.dynamic_index_in_dim(sliced, slot_of(b), 0, keepdims=True) for b in range(blocks)], axis=0
+    )
+    slab = lax.all_to_all(grouped, "grp", split_axis=0, concat_axis=2, tiled=True)
+    slab = jnp.transpose(slab, (1, 0, 2, 3))
+    tested = jnp.transpose(whole, (1, 3, 0, 2)).reshape(2 * funcs, -1)
 
     reduced = couple(green, slab, tested)
 
-    row_mine = [own_id == panel_order[q] for q in range(PANELS)]
-    col_mine = [panel_order[q] // slab_count == grp_index for q in range(PANELS)]
-    cols = jnp.stack([
-        jnp.where(
-            col_mine[q],
-            lax.dynamic_slice_in_dim(reduced, (panel_order[q] % slab_count) * funcs, funcs, 2),
-            0.0,
-        )
+    tiles = jnp.stack([
+        lax.dynamic_slice_in_dim(reduced, (panel_order[q] % slab_count) * funcs, funcs, 2)
         for q in range(PANELS)
     ])
-    pivots = jnp.stack([jnp.where(row_mine[q], cols, 0.0) for q in range(PANELS)])
-    pivots = lax.psum(pivots, ("blk", "grp"))
-    upper = lax.psum(jnp.stack([jnp.where(row_mine[q], reduced, 0.0) for q in range(PANELS)]), "blk")
-    cols = lax.psum(cols, "grp")
+    (spread,) = gather("grp", 2, tiles)
+    cols = jnp.stack([
+        lax.dynamic_index_in_dim(spread, panel_order[q] // slab_count, 0, keepdims=False)[q]
+        for q in range(PANELS)
+    ])
+    all_rows, all_cols = gather("blk", 3, reduced, cols)
+    places_of = [slot_of(panel_order[q]) for q in range(PANELS)]
+    upper = jnp.stack([lax.dynamic_index_in_dim(all_rows, p, 0, keepdims=False) for p in places_of])
+    pivots = jnp.stack([lax.dynamic_index_in_dim(all_cols, p, 0, keepdims=False) for p in places_of])
     first, joint, second = pivot_inverses(pivots)
     schur = update(reduced, upper, cols, pivots[1, 0], first, joint, second)
     return (reduced, schur)

time: 367 us -> 264 us (0.72)
  waiting for transfers between devices: 185 us -> 0.01 us
  Pallas kernels: 71.6 us -> 196 us
  blocking collectives: 31.3 us -> 0 us
  between operations: 38.4 us -> 26.7 us
  local copies, waits for them, and re-layouts: 20.9 us -> 27.4 us
    psum x3 -> x0, waiting for transfers between devices: 185 us -> none  [the longest x1 127 us: on_device(): pivots = lax.psum(pivots, ('blk', 'grp'))]
    pallas_call x0 -> x4, Pallas kernels: none -> 124 us  [gather(): pl.pallas_call(functools.partial(gather_kernel, axis, peers, count), in_s...]
    all_gather x1 -> x0, blocking collectives: 31.3 us -> none  [on_device(): own_full = lax.all_gather(basis_rows, 'grp', axis=2, tiled=True)[:, 0]]
    unnamed x17 -> x20, local copies, waits for them, and re-layouts: 12.9 us -> 14.5 us
  transfers between devices with their start and end apart: 5 -> 1, of which waited for: 2 -> 0; matrix products, arithmetic and copies ran while one was open for 3% -> 1% of each run, Pallas kernels for 17% -> 22%
where the time goes in v2:
time: 264 us; the launch traced here: 262 us
  Pallas kernels  196 us (74%)
  local copies, waits for them, and re-layouts  27.4 us (10%)
  between operations  26.7 us (10%)
  other arithmetic  6.01 us (2%)
  starting transfers between devices  4.76 us (2%)
    pallas_call x4, Pallas kernels, gather(): pl.pallas_call(functools.partial(gather_kernel, axis, peers, count), in_s...  124 us
    pallas_call x1, Pallas kernels, pivot_inverses(): pl.pallas_call(pivot_kernel, out_shape=(shape, shape, shape), compiler_pa...  37 us
    pallas_call x1, Pallas kernels, green_tiles(): pl.pallas_call(green_kernel, grid=(slab, unk // rows), in_specs=[pl.Block...  23.6 us
    unnamed x20, local copies, waits for them, and re-layouts  14.5 us
    pallas_call x1, Pallas kernels, update(): pl.pallas_call(update_kernel, out_shape=jax.ShapeDtypeStruct(full.shape,...  6.18 us
  transfers between devices with their start and end apart: 1, of which 0 were waited for; matrix products, arithmetic and copies ran while one was open for 1% of the time, Pallas kernels for 22%

profile of v2, /device:TPU:9, one launch (start us, length us, event | category | flops | bytes accessed | tf_op | source)
XLA Modules:
  0.0 262.5 jit_solution(3135637400548901999)
XLA Ops:
  0.6 1.2 slice_bitcast_fusion.1
  1.8 1.0 fusion.25
  2.8 1.4 fusion.26
  4.2 2.8 %fusion.21 = (s32[]{:T(128)}, s32[]{:T(128)}, s32[]{:T(128)}, s32[]{:T(128)}, s32[]{:T(128)}, /*index=5*/s32[]{:T(128)}, s32[]{:T(128)}, s32[]{:T(128)}, s32[]{:T(128)}, s32[]{:T(128)}) fusion(s32[8]{0:T(128)} %param.8, s32[]{:T(128)} %bitcast.16, s32[]{:T(128)} %bitcast.18), kind=kLoop, calls=%fused_computation.61 | loop fusion | flops 230 | bytes 80 | tf_op jit(solution)/shard_map/reduce_sum | solution.py:305
  16.9 1.3 fusion.2
  19.3 15.7 %gather_blk0.1 = bf16[8,2,256,128]{3,2,1,0:T(8,128)(2,1)} custom-call(bf16[2,256,128]{2,1,0:T(8,128)(2,1)} %pad_maximum_fusion.4.refs_0_), custom_call_target="tpu_custom_call" | custom-call | tf_op jit(solution)/shard_map/gather_blk0/pallas_call | solution.py:69
  35.6 1.6 dynamic-slice_dynamic-update-slice_fusion.7
  37.8 1.6 dynamic-slice_dynamic-update-slice_fusion.6
  40.0 1.6 dynamic-slice_dynamic-update-slice_fusion.5
  42.2 1.6 dynamic-slice_dynamic-update-slice_fusion.4
  44.5 1.6 dynamic-slice_dynamic-update-slice_fusion.3
  46.7 1.6 dynamic-slice_dynamic-update-slice_fusion.2
  48.9 1.6 dynamic-slice_dynamic-update-slice_fusion.1
  51.1 1.6 dynamic-slice_dynamic-update-slice_fusion
  52.7 4.8 %all-to-all-start = ((bf16[8,2,256,128]{3,2,1,0:T(8,128)(2,1)}), bf16[8,2,256,128]{3,2,1,0:T(8,128)(2,1)S(1)}, u32[]{:S(2)}, u32[]{:S(2)}) async-start(bf16[8,2,256,128]{3,2,1,0:T(8,128)(2,1)} %dynamic-slice_dynamic-update-slice_fusion), calls=%async_computation | async-start | bytes 2097152 | tf_op jit(solution)/shard_map/all_to_all | solution.py:310
  59.3 34.3 %gather_grp1.1 = bf16[4,2,256,128]{3,2,1,0:T(8,128)(2,1)} custom-call(bf16[2,256,128]{2,1,0:T(8,128)(2,1)} %pad_maximum_fusion.4.refs_0_), custom_call_target="tpu_custom_call" | custom-call | tf_op jit(solution)/shard_map/gather_grp1/pallas_call | solution.py:69
  102.0 1.0 copy.13
  103.0 1.3 copy.17
  106.4 23.6 %green.1.green_ref = bf16[2,1024,2048]{2,1,0:T(8,128)(2,1)} custom-call(f32[1024,3]{1,0:T(8,128)} %bitcast.51, f32[2,3,1024]{2,1,0:T(4,128)} %dynamic-slice_bitcast_fusion.5.basis_ref), custom_call_target="tpu_custom_call" | custom-call | flops 12582912000 | bytes 8388608 | tf_op jit(solution)/shard_map/green/pallas_call | solution.py:117
  130.1 3.4 %copy-done = bf16[2,1024,2048]{2,1,0:T(8,128)(2,1)S(1)} copy-done((bf16[2,1024,2048]{2,1,0:T(8,128)(2,1)S(1)}, bf16[2,1024,2048]{2,1,0:T(8,128)(2,1)}, u32[]{:S(2)}) %copy-start) | copy-done | bytes 8388632
  133.5 4.7 %couple.1.refs_0_.full_ref = f32[2,128,256]{2,1,0:T(8,128)} custom-call(bf16[2,1024,2048]{2,1,0:T(8,128)(2,1)S(1)} %copy-done, bf16[2,2,1024,128]{3,2,1,0:T(8,128)(2,1)S(1)} %bitcast.46, bf16[256,1024]{1,0:T(8,128)(2,1)S(1)} %bitcast.47), custom_call_target="tpu_custom_call" | custom-call | flops 2147483648 | bytes 8388608 | tf_op jit(solution)/shard_map/couple/pallas_call | solution.py:153
  138.2 1.0 dynamic-slice_bitcast_fusion.4
  139.2 0.7 pad_maximum_fusion.2.refs_0_
  139.9 24.7 %gather_grp2.1 = f32[4,2,2,128,128]{4,3,2,1,0:T(8,128)} custom-call(f32[2,2,128,128]{3,2,1,0:T(8,128)} %pad_maximum_fusion.2.refs_0_), custom_call_target="tpu_custom_call" | custom-call | tf_op jit(solution)/shard_map/gather_grp2/pallas_call | solution.py:69
  164.6 1.0 dynamic-slice_bitcast_fusion.2
  165.6 0.7 pad_maximum_fusion.3.refs_1_.cols_ref
  166.3 49.7 %gather_blk3.1 = (f32[8,2,128,256]{3,2,1,0:T(8,128)}, f32[8,2,2,128,128]{4,3,2,1,0:T(8,128)}) custom-call(f32[2,128,256]{2,1,0:T(8,128)} %couple.1.refs_0_.full_ref, f32[2,2,128,128]{3,2,1,0:T(8,128)} %pad_maximum_fusion.3.refs_1_.cols_ref), custom_call_target="tpu_custom_call" | custom-call | tf_op jit(solution)/shard_map/gather_blk3/pallas_call | solution.py:69
  216.0 0.9 dynamic-slice_bitcast_fusion.low_ref
  216.9 1.1 constant_dynamic-slice_fusion
  218.1 37.0 %pivots.1 = (f32[2,128,128]{2,1,0:T(8,128)S(1)}, f32[2,128,128]{2,1,0:T(8,128)S(1)}, f32[2,128,128]{2,1,0:T(8,128)S(1)}) custom-call(f32[2,2,2,128,128]{4,3,2,1,0:T(8,128)S(1)} %pad_maximum_fusion.1.d_ref), custom_call_target="tpu_custom_call" | custom-call | flops 20000000000 | bytes 1000000 | tf_op jit(solution)/shard_map/pivots/pallas_call | solution.py:245
  255.1 1.1 constant_dynamic-slice_fusion.3
  256.3 6.2 %update.1 = f32[2,128,256]{2,1,0:T(8,128)} custom-call(f32[2,128,256]{2,1,0:T(8,128)S(1)} %copy-done.1, f32[2,2,128,256]{3,2,1,0:T(8,128)S(1)} %pad_maximum_fusion.rows_ref, f32[2,2,128,128]{3,2,1,0:T(8,128)S(1)} %copy-done.2, f32[2,128,128]{2,1,0:T(8,128)S(1)} %dynamic-slice_bitcast_fusion.low_ref, f32[2,128,128]{2,1,0:T(8,128)S(1)} %get-tuple-element.9.first_ref, ...), custom_call_target="tpu_custom_call" | custom-call | flops 2000000000 | bytes 2000000 | tf_op jit(solution)/shard_map/update/pallas_call | solution.py:271
  (23 shorter events, 2.6 us)
Async XLA Ops:
  0.6 17.7 %copy-start.5 = (bf16[2,1,256,1024]{3,2,1,0:T(8,128)(2,1)S(1)}, bf16[2,1,256,1024]{3,2,1,0:T(8,128)(2,1)}, u32[]{:S(2)}) copy-start(bf16[2,1,256,1024]{3,2,1,0:T(8,128)(2,1)} %param.5) | copy-start | bytes 3145732
  35.6 21.8 %copy-start.4 = (s32[8]{0:T(128)S(1)}, s32[8]{0:T(128)}, u32[]{:S(2)}) copy-start(s32[8]{0:T(128)} %param.8) | copy-start | bytes 100
  42.2 59.6 %copy-start.3 = (s32[3,8,1024]{2,1,0:T(8,128)S(1)}, s32[3,8,1024]{2,1,0:T(8,128)}, u32[]{:S(2)}) copy-start(s32[3,8,1024]{2,1,0:T(8,128)} %param.7) | copy-start | bytes 294916
  52.7 77.3 %all-to-all-start = ((bf16[8,2,256,128]{3,2,1,0:T(8,128)(2,1)}), bf16[8,2,256,128]{3,2,1,0:T(8,128)(2,1)S(1)}, u32[]{:S(2)}, u32[]{:S(2)}) async-start(bf16[8,2,256,128]{3,2,1,0:T(8,128)(2,1)} %dynamic-slice_dynamic-update-slice_fusion), calls=%async_computation | async-start | bytes 2097152 | tf_op jit(solution)/shard_map/all_to_all | solution.py:310
  130.1 3.4 %copy-start = (bf16[2,1024,2048]{2,1,0:T(8,128)(2,1)S(1)}, bf16[2,1024,2048]{2,1,0:T(8,128)(2,1)}, u32[]{:S(2)}) copy-start(bf16[2,1024,2048]{2,1,0:T(8,128)(2,1)} %green.1.green_ref) | copy-start | bytes 25165828
  255.1 1.2 copy-start.1
  255.1 1.2 copy-start.2

commit v3 on v2

--- a/solution.py
+++ b/solution.py
@@ -297,16 +297,16 @@
     slab_pos = lax.dynamic_slice_in_dim(places, grp_index * slab_count, slab_count, 1)
     green = green_tiles(own_pos, jnp.transpose(slab_pos, (1, 0, 2)))
 
+    (whole,) = gather("grp", 1, basis_rows)
+    whole, basis_rows = lax.optimization_barrier((whole, basis_rows))
     (sliced,) = gather("blk", 0, basis_rows)
-    (whole,) = gather("grp", 1, basis_rows)
     slots = jnp.arange(blocks, dtype=jnp.int32)
 
     def slot_of(block):
         return jnp.sum(jnp.where(block_of_slot == block, slots, 0))
 
-    grouped = jnp.concatenate(
-        [lax.dynamic_index_in_dim(sliced, slot_of(b), 0, keepdims=True) for b in range(blocks)], axis=0
-    )
+    chosen = (block_of_slot[None, :] == slots[:, None])[:, :, None, None, None]
+    grouped = jnp.sum(jnp.where(chosen, sliced[None], 0), axis=1, dtype=jnp.float32).astype(jnp.bfloat16)
     slab = lax.all_to_all(grouped, "grp", split_axis=0, concat_axis=2, tiled=True)
     slab = jnp.transpose(slab, (1, 0, 2, 3))
     tested = jnp.transpose(whole, (1, 3, 0, 2)).reshape(2 * funcs, -1)

time: 264 us -> 221 us (0.84)
  Pallas kernels: 196 us -> 178 us
  between operations: 26.7 us -> 11.8 us
  local copies, waits for them, and re-layouts: 27.4 us -> 12.9 us
  other arithmetic: 6.01 us -> 10.5 us
    pallas_call x4, Pallas kernels: 124 us -> 106 us  [gather(): pl.pallas_call(functools.partial(gather_kernel, axis, peers, count), in_s...]
    unnamed x20 -> x15, local copies, waits for them, and re-layouts: 14.5 us -> 3.51 us
    reduce_sum x0 -> x1, other arithmetic: none -> 4.66 us  [on_device(): jnp.sum(jnp.where(chosen, sliced[None], 0), axis=1, dtype=jnp.float32)]
  transfers between devices with their start and end apart: 1 -> 1, of which waited for: 0 -> 0; matrix products, arithmetic and copies ran while one was open for 1% -> 2% of each run, Pallas kernels for 22% -> 11%
where the time goes in v3:
time: 221 us
  Pallas kernels  178 us (81%)
  local copies, waits for them, and re-layouts  12.9 us (6%)
  between operations  11.8 us (5%)
  other arithmetic  10.5 us (5%)
  starting transfers between devices  4.64 us (2%)
  matrix products  2.72 us (1%)
    pallas_call x4, Pallas kernels, gather(): pl.pallas_call(functools.partial(gather_kernel, axis, peers, count), in_s...  106 us
    pallas_call x1, Pallas kernels, pivot_inverses(): pl.pallas_call(pivot_kernel, out_shape=(shape, shape, shape), compiler_pa...  37 us
    pallas_call x1, Pallas kernels, green_tiles(): pl.pallas_call(green_kernel, grid=(slab, unk // rows), in_specs=[pl.Block...  23.7 us
    pallas_call x1, Pallas kernels, update(): pl.pallas_call(update_kernel, out_shape=jax.ShapeDtypeStruct(full.shape,...  6.18 us
    pallas_call x1, Pallas kernels, couple(): pl.pallas_call(couple_kernel, grid=(slab,), in_specs=[pl.BlockSpec((1, un...  4.7 us
    reduce_sum x1, other arithmetic, on_device(): jnp.sum(jnp.where(chosen, sliced[None], 0), axis=1, dtype=jnp.float32)  4.66 us
    all_to_all x1, starting transfers between devices, on_device(): lax.all_to_all(grouped, 'grp', split_axis=0, concat_axis=2, tiled=True)  4.64 us
  transfers between devices with their start and end apart: 1, of which 0 were waited for; matrix products, arithmetic and copies ran while one was open for 2% of the time, Pallas kernels for 11%

profile of v3, /device:TPU:9, one launch (start us, length us, event | category | flops | bytes accessed | tf_op | source)
XLA Modules:
  0.0 220.6 jit_solution(2585242602425031327)
XLA Ops:
  0.6 1.0 fusion.17
  1.6 1.1 slice_bitcast_fusion.1
  2.7 0.7 iota_compare_fusion
  3.4 1.3 fusion.2
  4.7 1.4 fusion.1
  6.1 0.7 pad_maximum_fusion.4.refs_0_
  6.8 15.2 %gather_grp1.1 = bf16[4,2,256,128]{3,2,1,0:T(8,128)(2,1)} custom-call(bf16[2,256,128]{2,1,0:T(8,128)(2,1)} %pad_maximum_fusion.4.refs_0_), custom_call_target="tpu_custom_call" | custom-call | tf_op jit(solution)/shard_map/gather_grp1/pallas_call | solution.py:69
  22.1 15.6 %gather_blk0.1 = bf16[8,2,256,128]{3,2,1,0:T(8,128)(2,1)} custom-call(bf16[2,256,128]{2,1,0:T(8,128)(2,1)} %pad_maximum_fusion.4.refs_0_), custom_call_target="tpu_custom_call" | custom-call | tf_op jit(solution)/shard_map/gather_blk0/pallas_call | solution.py:69
  37.7 4.7 %select_reduce_fusion = bf16[8,2,256,128]{3,2,1,0:T(8,128)(2,1)} fusion(pred[8,8]{1,0:T(8,128)(4,1)S(1)} %iota_compare_fusion, bf16[8,2,256,128]{3,2,1,0:T(8,128)(2,1)} %gather_blk0.1), kind=kLoop, calls=%fused_computation | loop fusion | flops 7864320 | bytes 2097216 | tf_op jit(solution)/shard_map/reduce_sum | solution.py:309
  42.4 4.6 %all-to-all-start = ((bf16[8,2,256,128]{3,2,1,0:T(8,128)(2,1)}), bf16[8,2,256,128]{3,2,1,0:T(8,128)(2,1)S(1)}, u32[]{:S(2)}, u32[]{:S(2)}) async-start(bf16[8,2,256,128]{3,2,1,0:T(8,128)(2,1)} %select_reduce_fusion), calls=%async_computation | async-start | bytes 2097152 | tf_op jit(solution)/shard_map/all_to_all | solution.py:310
  47.0 0.6 dynamic_slice.37
  48.9 0.6 fusion.18
  54.7 2.0 fusion.13
  59.9 1.0 copy.18
  61.0 0.3 copy.22
  61.3 0.1 copy.25
  62.7 0.6 dynamic-slice_bitcast_fusion.5.basis_ref
  63.3 23.7 %green.1.green_ref = bf16[2,1024,2048]{2,1,0:T(8,128)(2,1)} custom-call(f32[1024,3]{1,0:T(8,128)} %bitcast.51, f32[2,3,1024]{2,1,0:T(4,128)} %dynamic-slice_bitcast_fusion.5.basis_ref), custom_call_target="tpu_custom_call" | custom-call | flops 12582912000 | bytes 8388608 | tf_op jit(solution)/shard_map/green/pallas_call | solution.py:117
  87.0 0.1 copy.21
  87.1 3.4 %copy-done = bf16[2,1024,2048]{2,1,0:T(8,128)(2,1)S(1)} copy-done((bf16[2,1024,2048]{2,1,0:T(8,128)(2,1)S(1)}, bf16[2,1024,2048]{2,1,0:T(8,128)(2,1)}, u32[]{:S(2)}) %copy-start) | copy-done | bytes 8388632
  90.5 4.7 %couple.1.refs_0_.full_ref = f32[2,128,256]{2,1,0:T(8,128)} custom-call(bf16[2,1024,2048]{2,1,0:T(8,128)(2,1)S(1)} %copy-done, bf16[2,2,1024,128]{3,2,1,0:T(8,128)(2,1)S(1)} %bitcast.46, bf16[256,1024]{1,0:T(8,128)(2,1)S(1)} %bitcast.47), custom_call_target="tpu_custom_call" | custom-call | flops 2147483648 | bytes 8388608 | tf_op jit(solution)/shard_map/couple/pallas_call | solution.py:153
  95.2 1.0 dynamic-slice_bitcast_fusion.4
  96.1 0.7 pad_maximum_fusion.2.refs_0_
  96.9 26.4 %gather_grp2.1 = f32[4,2,2,128,128]{4,3,2,1,0:T(8,128)} custom-call(f32[2,2,128,128]{3,2,1,0:T(8,128)} %pad_maximum_fusion.2.refs_0_), custom_call_target="tpu_custom_call" | custom-call | tf_op jit(solution)/shard_map/gather_grp2/pallas_call | solution.py:69
  123.3 1.0 dynamic-slice_bitcast_fusion.2
  124.3 0.7 pad_maximum_fusion.3.refs_1_.cols_ref
  125.0 49.1 %gather_blk3.1 = (f32[8,2,128,256]{3,2,1,0:T(8,128)}, f32[8,2,2,128,128]{4,3,2,1,0:T(8,128)}) custom-call(f32[2,128,256]{2,1,0:T(8,128)} %couple.1.refs_0_.full_ref, f32[2,2,128,128]{3,2,1,0:T(8,128)} %pad_maximum_fusion.3.refs_1_.cols_ref), custom_call_target="tpu_custom_call" | custom-call | tf_op jit(solution)/shard_map/gather_blk3/pallas_call | solution.py:69
  174.1 0.9 dynamic-slice_bitcast_fusion.low_ref
  175.0 1.1 constant_dynamic-slice_fusion
  176.1 1.1 constant_dynamic-slice_fusion.3
  177.3 37.0 %pivots.1 = (f32[2,128,128]{2,1,0:T(8,128)S(1)}, f32[2,128,128]{2,1,0:T(8,128)S(1)}, f32[2,128,128]{2,1,0:T(8,128)S(1)}) custom-call(f32[2,2,2,128,128]{4,3,2,1,0:T(8,128)S(1)} %pad_maximum_fusion.1.d_ref), custom_call_target="tpu_custom_call" | custom-call | flops 20000000000 | bytes 1000000 | tf_op jit(solution)/shard_map/pivots/pallas_call | solution.py:245
  214.4 6.2 %update.1 = f32[2,128,256]{2,1,0:T(8,128)} custom-call(f32[2,128,256]{2,1,0:T(8,128)S(1)} %copy-done.1, f32[2,2,128,256]{3,2,1,0:T(8,128)S(1)} %pad_maximum_fusion.rows_ref, f32[2,2,128,128]{3,2,1,0:T(8,128)S(1)} %copy-done.2, f32[2,128,128]{2,1,0:T(8,128)S(1)} %dynamic-slice_bitcast_fusion.low_ref, f32[2,128,128]{2,1,0:T(8,128)S(1)} %get-tuple-element.13.first_ref, ...), custom_call_target="tpu_custom_call" | custom-call | flops 2000000000 | bytes 2000000 | tf_op jit(solution)/shard_map/update/pallas_call | solution.py:271
  (19 shorter events, 0.2 us)
Async XLA Ops:
  4.7 42.3 %copy-start.6 = (s32[8]{0:T(128)S(1)}, s32[8]{0:T(128)}, u32[]{:S(2)}) copy-start(s32[8]{0:T(128)} %param.8) | copy-start | bytes 100
  4.7 44.2 %copy-start.5 = (s32[8]{0:T(128)S(1)}, s32[8]{0:T(128)}, u32[]{:S(2)}) copy-start(s32[8]{0:T(128)} %param.9) | copy-start | bytes 100
  4.7 55.1 %copy-start.4 = (s32[3,8,1024]{2,1,0:T(8,128)S(1)}, s32[3,8,1024]{2,1,0:T(8,128)}, u32[]{:S(2)}) copy-start(s32[3,8,1024]{2,1,0:T(8,128)} %param.7) | copy-start | bytes 294916
  22.1 38.9 %copy-start.3 = (bf16[4,2,256,128]{3,2,1,0:T(8,128)(2,1)S(1)}, bf16[4,2,256,128]{3,2,1,0:T(8,128)(2,1)}, u32[]{:S(2)}) copy-start(bf16[4,2,256,128]{3,2,1,0:T(8,128)(2,1)} %gather_grp1.1) | copy-start | bytes 1572868
  42.4 44.6 %all-to-all-start = ((bf16[8,2,256,128]{3,2,1,0:T(8,128)(2,1)}), bf16[8,2,256,128]{3,2,1,0:T(8,128)(2,1)S(1)}, u32[]{:S(2)}, u32[]{:S(2)}) async-start(bf16[8,2,256,128]{3,2,1,0:T(8,128)(2,1)} %select_reduce_fusion), calls=%async_computation | async-start | bytes 2097152 | tf_op jit(solution)/shard_map/all_to_all | solution.py:310
  87.1 3.4 %copy-start = (bf16[2,1024,2048]{2,1,0:T(8,128)(2,1)S(1)}, bf16[2,1024,2048]{2,1,0:T(8,128)(2,1)}, u32[]{:S(2)}) copy-start(bf16[2,1024,2048]{2,1,0:T(8,128)(2,1)} %green.1.green_ref) | copy-start | bytes 25165828
  177.2 37.1 %copy-start.1 = (f32[2,128,256]{2,1,0:T(8,128)S(1)}, f32[2,128,256]{2,1,0:T(8,128)}, u32[]{:S(2)}) copy-start(f32[2,128,256]{2,1,0:T(8,128)} %couple.1.refs_0_.full_ref) | copy-start | bytes 786436
  177.3 37.1 %copy-start.2 = (f32[2,2,128,128]{3,2,1,0:T(8,128)S(1)}, f32[2,2,128,128]{3,2,1,0:T(8,128)}, u32[]{:S(2)}) copy-start(f32[2,2,128,128]{3,2,1,0:T(8,128)} %pad_maximum_fusion.3.refs_1_.cols_ref) | copy-start | bytes 786436

commit v4 on v3

--- a/solution.py
+++ b/solution.py
@@ -312,6 +312,7 @@
     tested = jnp.transpose(whole, (1, 3, 0, 2)).reshape(2 * funcs, -1)
 
     reduced = couple(green, slab, tested)
+    all_rows = lax.all_gather(reduced, "blk")
 
     tiles = jnp.stack([
         lax.dynamic_slice_in_dim(reduced, (panel_order[q] % slab_count) * funcs, funcs, 2)
@@ -322,7 +323,7 @@
         lax.dynamic_index_in_dim(spread, panel_order[q] // slab_count, 0, keepdims=False)[q]
         for q in range(PANELS)
     ])
-    all_rows, all_cols = gather("blk", 3, reduced, cols)
+    (all_cols,) = gather("blk", 3, cols)
     places_of = [slot_of(panel_order[q]) for q in range(PANELS)]
     upper = jnp.stack([lax.dynamic_index_in_dim(all_rows, p, 0, keepdims=False) for p in places_of])
     pivots = jnp.stack([lax.dynamic_index_in_dim(all_cols, p, 0, keepdims=False) for p in places_of])

time: 221 us -> 211 us (0.955)
  Pallas kernels: 178 us -> 155 us
  between operations: 11.8 us -> 24.8 us
    pallas_call x4, Pallas kernels: 106 us -> 83.7 us  [gather(): pl.pallas_call(functools.partial(gather_kernel, axis, peers, count), in_s...]
  transfers between devices with their start and end apart: 1 -> 2, of which waited for: 0 -> 0; matrix products, arithmetic and copies ran while one was open for 2% -> 5% of each run, Pallas kernels for 11% -> 54%
where the time goes in v4:
time: 211 us
  Pallas kernels  155 us (73%)
  between operations  24.8 us (12%)
  local copies, waits for them, and re-layouts  12.9 us (6%)
  other arithmetic  10.4 us (5%)
  starting transfers between devices  4.64 us (2%)
  matrix products  2.73 us (1%)
    pallas_call x4, Pallas kernels, gather(): pl.pallas_call(functools.partial(gather_kernel, axis, peers, count), in_s...  83.7 us
    pallas_call x1, Pallas kernels, pivot_inverses(): pl.pallas_call(pivot_kernel, out_shape=(shape, shape, shape), compiler_pa...  37 us
    pallas_call x1, Pallas kernels, green_tiles(): pl.pallas_call(green_kernel, grid=(slab, unk // rows), in_specs=[pl.Block...  23.7 us
    pallas_call x1, Pallas kernels, update(): pl.pallas_call(update_kernel, out_shape=jax.ShapeDtypeStruct(full.shape,...  6.18 us
    pallas_call x1, Pallas kernels, couple(): pl.pallas_call(couple_kernel, grid=(slab,), in_specs=[pl.BlockSpec((1, un...  4.71 us
    reduce_sum x1, other arithmetic, on_device(): jnp.sum(jnp.where(chosen, sliced[None], 0), axis=1, dtype=jnp.float32)  4.65 us
    all_to_all x1, starting transfers between devices, on_device(): lax.all_to_all(grouped, 'grp', split_axis=0, concat_axis=2, tiled=True)  4.64 us
  transfers between devices with their start and end apart: 2, of which 0 were waited for; matrix products, arithmetic and copies ran while one was open for 5% of the time, Pallas kernels for 54%

profile of v4, /device:TPU:9, one launch (start us, length us, event | category | flops | bytes accessed | tf_op | source)
XLA Modules:
  0.0 210.8 jit_solution(13918745836466878103)
XLA Ops:
  7.2 1.0 fusion.17
  8.2 1.1 slice_bitcast_fusion.1
  9.2 0.7 iota_compare_fusion
  9.9 1.3 fusion.2
  11.3 1.4 fusion.1
  12.7 0.7 pad_maximum_fusion.4.refs_0_
  13.4 15.2 %gather_grp1.1 = bf16[4,2,256,128]{3,2,1,0:T(8,128)(2,1)} custom-call(bf16[2,256,128]{2,1,0:T(8,128)(2,1)} %pad_maximum_fusion.4.refs_0_), custom_call_target="tpu_custom_call" | custom-call | tf_op jit(solution)/shard_map/gather_grp1/pallas_call | solution.py:69
  28.6 15.6 %gather_blk0.1 = bf16[8,2,256,128]{3,2,1,0:T(8,128)(2,1)} custom-call(bf16[2,256,128]{2,1,0:T(8,128)(2,1)} %pad_maximum_fusion.4.refs_0_), custom_call_target="tpu_custom_call" | custom-call | tf_op jit(solution)/shard_map/gather_blk0/pallas_call | solution.py:69
  44.2 4.7 %select_reduce_fusion = bf16[8,2,256,128]{3,2,1,0:T(8,128)(2,1)} fusion(pred[8,8]{1,0:T(8,128)(4,1)S(1)} %iota_compare_fusion, bf16[8,2,256,128]{3,2,1,0:T(8,128)(2,1)} %gather_blk0.1), kind=kLoop, calls=%fused_computation | loop fusion | flops 7864320 | bytes 2097216 | tf_op jit(solution)/shard_map/reduce_sum | solution.py:309
  48.9 4.6 %all-to-all-start = ((bf16[8,2,256,128]{3,2,1,0:T(8,128)(2,1)}), bf16[8,2,256,128]{3,2,1,0:T(8,128)(2,1)S(1)}, u32[]{:S(2)}, u32[]{:S(2)}) async-start(bf16[8,2,256,128]{3,2,1,0:T(8,128)(2,1)} %select_reduce_fusion), calls=%async_computation | async-start | bytes 2097152 | tf_op jit(solution)/shard_map/all_to_all | solution.py:310
  53.5 0.6 dynamic_slice.37
  56.1 0.1 copy_convert_fusion
  56.2 1.0 copy.24
  57.2 0.3 copy.28
  57.5 0.1 copy.31
  57.6 0.6 dynamic-slice_bitcast_fusion.5.basis_ref
  58.2 23.7 %green.1.green_ref = bf16[2,1024,2048]{2,1,0:T(8,128)(2,1)} custom-call(f32[1024,3]{1,0:T(8,128)} %bitcast.52, f32[2,3,1024]{2,1,0:T(4,128)} %dynamic-slice_bitcast_fusion.5.basis_ref), custom_call_target="tpu_custom_call" | custom-call | flops 12582912000 | bytes 8388608 | tf_op jit(solution)/shard_map/green/pallas_call | solution.py:117
  82.0 3.4 %copy-done = bf16[2,1024,2048]{2,1,0:T(8,128)(2,1)S(1)} copy-done((bf16[2,1024,2048]{2,1,0:T(8,128)(2,1)S(1)}, bf16[2,1024,2048]{2,1,0:T(8,128)(2,1)}, u32[]{:S(2)}) %copy-start) | copy-done | bytes 8388632
  85.4 4.7 %couple.1.full_ref = f32[2,128,256]{2,1,0:T(8,128)} custom-call(bf16[2,1024,2048]{2,1,0:T(8,128)(2,1)S(1)} %copy-done, bf16[2,2,1024,128]{3,2,1,0:T(8,128)(2,1)S(1)} %bitcast.47, bf16[256,1024]{1,0:T(8,128)(2,1)S(1)} %bitcast.48), custom_call_target="tpu_custom_call" | custom-call | flops 2147483648 | bytes 8388608 | tf_op jit(solution)/shard_map/couple/pallas_call | solution.py:153
  90.1 0.6 fusion.18
  95.5 1.9 fusion.13
  101.1 1.0 dynamic-slice_bitcast_fusion.4
  102.1 0.7 pad_maximum_fusion.2.refs_0_
  102.9 26.4 %gather_grp2.1 = f32[4,2,2,128,128]{4,3,2,1,0:T(8,128)} custom-call(f32[2,2,128,128]{3,2,1,0:T(8,128)} %pad_maximum_fusion.2.refs_0_), custom_call_target="tpu_custom_call" | custom-call | tf_op jit(solution)/shard_map/gather_grp2/pallas_call | solution.py:69
  129.3 1.0 dynamic-slice_bitcast_fusion.2
  130.3 0.7 pad_maximum_fusion.3.refs_0_.cols_ref
  131.0 26.5 %gather_blk3.1 = f32[8,2,2,128,128]{4,3,2,1,0:T(8,128)} custom-call(f32[2,2,128,128]{3,2,1,0:T(8,128)} %pad_maximum_fusion.3.refs_0_.cols_ref), custom_call_target="tpu_custom_call" | custom-call | tf_op jit(solution)/shard_map/gather_blk3/pallas_call | solution.py:69
  157.5 0.9 dynamic-slice_bitcast_fusion.low_ref
  158.4 1.1 constant_dynamic-slice_fusion
  159.6 37.0 %pivots.1 = (f32[2,128,128]{2,1,0:T(8,128)S(1)}, f32[2,128,128]{2,1,0:T(8,128)S(1)}, f32[2,128,128]{2,1,0:T(8,128)S(1)}) custom-call(f32[2,2,2,128,128]{4,3,2,1,0:T(8,128)S(1)} %pad_maximum_fusion.1.d_ref), custom_call_target="tpu_custom_call" | custom-call | flops 20000000000 | bytes 1000000 | tf_op jit(solution)/shard_map/pivots/pallas_call | solution.py:245
  196.6 1.1 constant_dynamic-slice_fusion.3
  197.8 6.2 %update.1 = f32[2,128,256]{2,1,0:T(8,128)} custom-call(f32[2,128,256]{2,1,0:T(8,128)S(1)} %copy-done.1, f32[2,2,128,256]{3,2,1,0:T(8,128)S(1)} %pad_maximum_fusion.rows_ref, f32[2,2,128,128]{3,2,1,0:T(8,128)S(1)} %copy-done.2, f32[2,128,128]{2,1,0:T(8,128)S(1)} %dynamic-slice_bitcast_fusion.low_ref, f32[2,128,128]{2,1,0:T(8,128)S(1)} %get-tuple-element.9.first_ref, ...), custom_call_target="tpu_custom_call" | custom-call | flops 2000000000 | bytes 2000000 | tf_op jit(solution)/shard_map/update/pallas_call | solution.py:271
  (22 shorter events, 0.2 us)
Async XLA Ops:
  11.2 42.3 %copy-start.6 = (s32[8]{0:T(128)S(1)}, s32[8]{0:T(128)}, u32[]{:S(2)}) copy-start(s32[8]{0:T(128)} %param.8) | copy-start | bytes 100
  11.3 44.8 %copy-start.4 = (s32[3,8,1024]{2,1,0:T(8,128)S(1)}, s32[3,8,1024]{2,1,0:T(8,128)}, u32[]{:S(2)}) copy-start(s32[3,8,1024]{2,1,0:T(8,128)} %param.7) | copy-start | bytes 294916
  28.6 28.6 %copy-start.3 = (bf16[4,2,256,128]{3,2,1,0:T(8,128)(2,1)S(1)}, bf16[4,2,256,128]{3,2,1,0:T(8,128)(2,1)}, u32[]{:S(2)}) copy-start(bf16[4,2,256,128]{3,2,1,0:T(8,128)(2,1)} %gather_grp1.1) | copy-start | bytes 1572868
  48.9 33.0 %all-to-all-start = ((bf16[8,2,256,128]{3,2,1,0:T(8,128)(2,1)}), bf16[8,2,256,128]{3,2,1,0:T(8,128)(2,1)S(1)}, u32[]{:S(2)}, u32[]{:S(2)}) async-start(bf16[8,2,256,128]{3,2,1,0:T(8,128)(2,1)} %select_reduce_fusion), calls=%async_computation | async-start | bytes 2097152 | tf_op jit(solution)/shard_map/all_to_all | solution.py:310
  53.5 143.1 %all-gather.3.cloned.1.call-start = ((), (), s32[]{:S(2)}) async-start(), calls=%async_computation.1 | async-start | bytes 2359296 | tf_op jit(solution)/shard_map/all_gather | solution.py:315
  82.0 3.4 %copy-start = (bf16[2,1024,2048]{2,1,0:T(8,128)(2,1)S(1)}, bf16[2,1024,2048]{2,1,0:T(8,128)(2,1)}, u32[]{:S(2)}) copy-start(bf16[2,1024,2048]{2,1,0:T(8,128)(2,1)} %green.1.green_ref) | copy-start | bytes 25165828
  85.4 4.7 %copy-start.5 = (s32[8]{0:T(128)S(1)}, s32[8]{0:T(128)}, u32[]{:S(2)}) copy-start(s32[8]{0:T(128)} %param.9) | copy-start | bytes 100
  159.5 38.2 %copy-start.1 = (f32[2,128,256]{2,1,0:T(8,128)S(1)}, f32[2,128,256]{2,1,0:T(8,128)}, u32[]{:S(2)}) copy-start(f32[2,128,256]{2,1,0:T(8,128)} %couple.1.full_ref) | copy-start | bytes 786436
  159.5 38.2 %copy-start.2 = (f32[2,2,128,128]{3,2,1,0:T(8,128)S(1)}, f32[2,2,128,128]{3,2,1,0:T(8,128)}, u32[]{:S(2)}) copy-start(f32[2,2,128,128]{3,2,1,0:T(8,128)} %pad_maximum_fusion.3.refs_0_.cols_ref) | copy-start | bytes 786436
Sparse Core Ops, SparseCore 0:
  90.2 28.6 all-gather.2
